TPU v7x, 128 devices: a whole 4x4x4 slice. The times are simulated.
128 devices in a mesh: tm: 32 (over z, x, y_hi), rows: 4 (over y_lo, core).
Axes of the slice: x: 4, y: 4 (y_hi: 2, y_lo: 2; y = y_hi * 2 + y_lo), z: 4, core: 2. Of those that a mesh axis runs over, the one named last changes fastest.
Arguments:
- video: bfloat16 [256, 32, 128, 128], P('tm', 'rows'), may hold values from -36 to 50
- conv_weight: bfloat16 [3, 3, 3, 128, 256], replicated, may hold values from -0.109375 to 0.109375
- norm_gain: float32 [256], replicated, may hold values from 0.5 to 1.5
- norm_bias: float32 [256], replicated, may hold values from -3 to 3
Outputs:
- patch_tokens: bfloat16 [16, 64, 256, 1024], P('rows', 'tm')
All inputs are finite; a program needn't handle non-finite values.
Results may differ from a plain program's by a relative error of at most 0.0049.
Values may be sent and summed in bfloat16 or wider, within the bound.
A program may use at most 128 MiB of HBM per device.

v0:
```python
import jax
import jax.numpy as jnp
from jax import lax
from jax.sharding import PartitionSpec as P

GROUPS = 32
inv_root = 0.7071067811865476


def from_partner(block, axis, distance):
    count = lax.axis_size(axis)
    route = []
    for low in range(count):
        high = low | 1 << distance
        if high != low and high < count:
            route += [(low, high), (high, low)]
    return lax.ppermute(block, axis, route)


def shifted(block, axis, distance):
    devices = range(lax.axis_size(axis))
    route = [(i - distance, i) for i in devices if i - distance in devices]
    return lax.ppermute(block, axis, route)


def padded_2(cells, sides, width):
    for axis, dim in sides:
        count = lax.axis_size(axis)
        ends = count - 1
        head = lax.slice_in_dim(cells, 0, width, axis=dim)
        tail = lax.slice_in_dim(cells, cells.shape[dim] - width, cells.shape[dim], axis=dim)
        cells = jnp.concatenate(
            [
                lax.ppermute(tail, axis, [(i, (i + 1) % count) for i in range(ends)]),
                cells,
                lax.ppermute(head, axis, [((i + 1) % count, i) for i in range(ends)]),
            ],
            axis=dim,
        )
    return cells


def per_device(video, conv_weight, norm_gain, norm_bias):
    frames, height, width, channels = video.shape
    tm_count = lax.axis_size("tm")
    current = video.astype(jnp.float32)
    position = lax.axis_index("tm")
    for bit_number in range(3):
        partner = from_partner(current, "tm", bit_number)
        is_upper = position >> bit_number & 1 == 1
        current = jnp.where(
            is_upper, (partner - current) * inv_root, (current + partner) * inv_root
        )
    wavelet = current.astype(jnp.bfloat16)
    last_frames = wavelet[frames - 2 :]
    earlier = shifted(last_frames, "tm", 1)
    extended = jnp.concatenate([earlier, wavelet], axis=0)
    with_rows = padded_2(extended, (("rows", 1),), 1)
    padded = jnp.pad(with_rows, ((0, 0), (0, 0), (1, 1), (0, 0)))
    convolved = lax.conv_general_dilated(
        padded[None],
        conv_weight,
        (1, 1, 1),
        "VALID",
        dimension_numbers=("NDHWC", "DHWIO", "NDHWC"),
        preferred_element_type=jnp.float32,
    )[0]
    out_frames, out_height, out_width, out_channels = convolved.shape
    group_count = GROUPS
    groups = convolved.reshape(
        out_frames, out_height, out_width, group_count, out_channels // group_count
    )
    entries = float(
        out_frames
        * out_height
        * out_width
        * (out_channels // group_count)
        * tm_count
        * lax.axis_size("rows")
    )
    local_sums = jnp.sum(groups, axis=(0, 1, 2, 4))
    group_total = lax.psum(local_sums, ("tm", "rows"))
    group_mean = group_total / entries
    centered = groups - group_mean[:, None]
    squares = lax.psum(jnp.sum(centered * centered, axis=(0, 1, 2, 4)), ("tm", "rows"))
    variance = squares / entries
    normed = (centered / jnp.sqrt(variance + 1e-05)[:, None]).reshape(
        out_frames, out_height, out_width, out_channels
    )
    activated = jax.nn.silu(normed * norm_gain + norm_bias).astype(jnp.bfloat16)
    arranged = activated.reshape(
        out_frames, out_height // 2, 2, out_width // 2, 2, out_channels
    ).transpose(1, 3, 0, 2, 4, 5)
    arranged = arranged.reshape(out_height // 2, out_width // 2, out_frames, 4 * out_channels)
    return lax.all_to_all(arranged, "tm", split_axis=1, concat_axis=2, tiled=True)


def solution(mesh):
    placed = (P("tm", "rows", None, None), P(), P(), P())
    return jax.shard_map(
        per_device,
        mesh=mesh,
        in_specs=placed,
        out_specs=P("rows", "tm", None, None),
        check_vma=False,
    )
```

profile of v0, /device:TPU:0, one launch (start us, length us, event | category | flops | bytes accessed | tf_op | source)
XLA Modules:
  0.0 597.1 jit_solution(17662172223809165032)
XLA Ops:
  0.0 0.0 copy-start
  0.0 4.3 convert_element_type.12
  4.3 3.3 collective-permute-start
  7.5 90.9 %collective-permute-done = f32[8,8,128,128]{3,2,1,0:T(8,128)} collective-permute-done((f32[8,8,128,128]{3,2,1,0:T(8,128)}, f32[8,8,128,128]{3,2,1,0:T(8,128)}, u32[]{:S(2)}, u32[]{:S(2)}) %collective-permute-start) | collective-permute-done | bytes 4194336 | tf_op jit(solution)/shard_map/ppermute | solution.py:17
  98.4 5.9 multiply_select_fusion.1
  104.3 1.5 collective-permute-start.1
  105.9 90.2 %collective-permute-done.1 = f32[8,8,128,128]{3,2,1,0:T(8,128)} collective-permute-done((f32[8,8,128,128]{3,2,1,0:T(8,128)}, f32[8,8,128,128]{3,2,1,0:T(8,128)}, u32[]{:S(2)}, u32[]{:S(2)}) %collective-permute-start.1) | collective-permute-done | bytes 4194336 | tf_op jit(solution)/shard_map/ppermute | solution.py:17
  196.1 6.9 %multiply_select_fusion = f32[8,8,128,128]{3,2,1,0:T(8,128)} fusion(f32[8,8,128,128]{3,2,1,0:T(8,128)} %multiply_select_fusion.1, f32[8,8,128,128]{3,2,1,0:T(8,128)} %collective-permute-done.1, pred[]{:T(512)S(6)} %eq.10), kind=kLoop, calls=%fused_computation.15 | loop fusion | flops 5242880 | bytes 12582913 | tf_op jit(solution)/shard_map/jit(_where)/select_n | solution.py:51
  203.0 3.0 collective-permute-start.2
  206.1 89.3 %collective-permute-done.2 = f32[8,8,128,128]{3,2,1,0:T(8,128)} collective-permute-done((f32[8,8,128,128]{3,2,1,0:T(8,128)}, f32[8,8,128,128]{3,2,1,0:T(8,128)}, u32[]{:S(2)}, u32[]{:S(2)}) %collective-permute-start.2) | collective-permute-done | bytes 4194336 | tf_op jit(solution)/shard_map/ppermute | solution.py:17
  295.4 4.5 select_convert_fusion
  299.9 5.1 collective-permute-start.3
  305.1 8.4 %collective-permute-done.3 = bf16[2,8,128,128]{3,2,1,0:T(8,128)(2,1)S(1)} collective-permute-done((bf16[2,8,128,128]{3,2,1,0:T(8,128)(2,1)S(1)}, bf16[2,8,128,128]{3,2,1,0:T(8,128)(2,1)S(1)}, u32[]{:S(2)}, u32[]{:S(2)}) %collective-permute-start.3) | collective-permute-done | bytes 524320 | tf_op jit(solution)/shard_map/ppermute | solution.py:23
  313.5 0.1 pad_maximum_fusion.1
  313.5 1.3 collective-permute-start.4
  314.9 1.3 collective-permute-start.5
  316.2 0.0 collective-permute-done.4
  316.2 3.1 collective-permute-done.5
  319.3 2.1 fusion.13
  321.4 2.0 pad.5
  323.4 6.9 %reshape.19 = bf16[10,10,1,8,17,128]{5,4,3,1,0,2:T(8,128)(2,1)} reshape(bf16[10,10,1,136,128]{4,3,1,0,2:T(8,128)(2,1)} %pad.5) | data formatting | bytes 6963200 | tf_op jit(solution)/shard_map/conv_general_dilated | solution.py:60
  330.4 3.0 copy.29
  333.4 0.1 slice.15
  333.5 0.0 copy-done
  333.5 0.0 copy-done.3
  333.5 19.0 %select_reduce_fusion.1 = (f32[256]{0:T(256)S(1)}, f32[8,8,8,17,256]{4,2,3,1,0:T(8,128)}) fusion(pred[8,17]{0,1:T(8,128)(4,1)S(1)} %copy-done.3, bf16[3,3,3,128,256]{4,3,2,1,0:T(8,128)(2,1)S(1)} %copy-done, bf16[10,10,1,7,2,128]{5,3,4,1,0,2:T(8,128)(2,1)S(1)} %slice.15, bf16[10,10,1,8,17,128]{5,3,4,1,0,2:T(8,128)(2,1)S(1)} %copy.29), kind=kOutput, calls=%fused_computation.3 | convolution fusion | flops 15419842560 | bytes 14523528 | tf_op jit(solution)/shard_map/conv_general_dilated | solution.py:60
  352.6 0.1 reduce_sum.24
  352.7 0.1 reduce_sum.25
  352.8 75.9 %psum.14 = f32[32]{0:T(128)S(1)} all-reduce(f32[32]{0:T(128)S(1)} %reduce_sum.25), channel_id=1, replica_groups=mesh['tm'=32,'rows'=4] {'tm','rows'}, use_global_device_ids=true, to_apply=%region_2.3 | all-reduce | flops 32 | bytes 256 | tf_op jit(solution)/shard_map/psum | solution.py:82
  428.7 0.1 sub.31
  428.8 0.1 sub.32
  428.8 0.0 copy-start.2
  428.9 6.3 %copy.30 = f32[8,8,8,17,256]{4,1,3,2,0:T(8,128)S(1)} copy(f32[8,8,8,17,256]{4,2,3,1,0:T(8,128)} %get-tuple-element.8) | data formatting | bytes 17825792 | tf_op jit(solution)/shard_map/conv_general_dilated | solution.py:60
  435.2 1.5 select_reduce_fusion
  436.8 4.1 slice.16
  440.8 0.1 reduce_sum.36
  440.9 0.1 reduce_sum.37
  441.0 0.0 copy-start.4
  441.0 0.0 copy-start.5
  441.0 11.5 %copy.31 = f32[8,8,1,128,256]{4,0,3,1,2:T(8,128)} copy(f32[8,8,1,128,256]{4,1,3,0,2:T(8,128)} %slice.16) | data formatting | bytes 16777216 | tf_op jit(solution)/shard_map/conv_general_dilated | solution.py:60
  452.5 62.4 %psum.15 = f32[32]{0:T(128)S(1)} all-reduce(f32[32]{0:T(128)S(1)} %reduce_sum.37), channel_id=1, replica_groups=mesh['tm'=32,'rows'=4] {'tm','rows'}, use_global_device_ids=true, to_apply=%region_5.6 | all-reduce | flops 32 | bytes 256 | tf_op jit(solution)/shard_map/psum | solution.py:85
  515.0 0.1 div.27
  515.0 0.1 div.28
  515.2 6.9 %fusion.5 = bf16[4,64,8,2,2,256]{5,1,4,3,0,2:T(8,128)(2,1)S(1)} fusion(f32[256]{0:T(256)S(1)} %copy-done.4, f32[256]{0:T(256)S(1)} %copy-done.5, f32[256]{0:T(256)S(1)} %div.28, f32[256]{0:T(256)S(1)} %sub.32, f32[8,4,2,64,2,256]{5,0,4,3,2,1:T(8,128)} %bitcast.27), kind=kLoop, calls=%fused_computation.17 | loop fusion | flops 18874368 | bytes 12587008 | tf_op jit(solution)/shard_map/transpose | solution.py:93
  522.0 6.4 %copy.37 = bf16[4,64,8,2,2,256]{5,4,3,2,0,1:T(2,128)(2,1)} copy(bf16[4,64,8,2,2,256]{5,1,4,3,0,2:T(8,128)(2,1)S(1)} %fusion.5) | data formatting | bytes 8388608 | tf_op jit(solution)/shard_map/reshape | solution.py:94
  528.4 7.7 %reshape.33 = bf16[4,64,8,1024]{3,2,0,1:T(8,128)(2,1)} reshape(bf16[4,64,8,2,2,256]{5,4,3,2,0,1:T(2,128)(2,1)} %copy.37) | data formatting | bytes 8388608 | tf_op jit(solution)/shard_map/reshape | solution.py:94
  536.1 58.5 %all_to_all.18 = bf16[4,64,8,1024]{3,2,0,1:T(8,128)(2,1)S(1)} all-to-all(bf16[4,64,8,1024]{3,2,0,1:T(8,128)(2,1)} %reshape.33), channel_id=1, replica_groups=mesh['tm'=32,'rows'=4] {'tm'}, dimensions={1} | all-to-all | bytes 8388608 | tf_op jit(solution)/shard_map/all_to_all | solution.py:95
  594.6 2.5 copy.52
  (9 shorter events, 0.1 us)
Async XLA Ops:
  0.0 333.5 %copy-start = (bf16[3,3,3,128,256]{4,3,2,1,0:T(8,128)(2,1)S(1)}, bf16[3,3,3,128,256]{4,3,2,1,0:T(8,128)(2,1)}, u32[]{:S(2)}) copy-start(bf16[3,3,3,128,256]{4,3,2,1,0:T(8,128)(2,1)} %param.5) | copy-start | bytes 5308420
  4.3 94.2 %collective-permute-start = (f32[8,8,128,128]{3,2,1,0:T(8,128)}, f32[8,8,128,128]{3,2,1,0:T(8,128)}, u32[]{:S(2)}, u32[]{:S(2)}) collective-permute-start(f32[8,8,128,128]{3,2,1,0:T(8,128)} %convert_element_type.12), channel_id=1, source_target_pairs={{0,4},{4,0},{8,12},{12,8},{16,20},{20,16},{24,28},{28,24},{32,36},... | collective-permute-start | bytes 12582920 | tf_op jit(solution)/shard_map/ppermute | solution.py:17
  104.3 91.8 %collective-permute-start.1 = (f32[8,8,128,128]{3,2,1,0:T(8,128)}, f32[8,8,128,128]{3,2,1,0:T(8,128)}, u32[]{:S(2)}, u32[]{:S(2)}) collective-permute-start(f32[8,8,128,128]{3,2,1,0:T(8,128)} %multiply_select_fusion.1), channel_id=1, source_target_pairs={{0,8},{8,0},{4,12},{12,4},{16,24},{24,16},{20,28},{28,20},{32,40},... | collective-permute-start | bytes 12582920 | tf_op jit(solution)/shard_map/ppermute | solution.py:17
  203.0 92.4 %collective-permute-start.2 = (f32[8,8,128,128]{3,2,1,0:T(8,128)}, f32[8,8,128,128]{3,2,1,0:T(8,128)}, u32[]{:S(2)}, u32[]{:S(2)}) collective-permute-start(f32[8,8,128,128]{3,2,1,0:T(8,128)} %multiply_select_fusion), channel_id=1, source_target_pairs={{0,16},{16,0},{4,20},{20,4},{8,24},{24,8},{12,28},{28,12},{32,48},... | collective-permute-start | bytes 12582920 | tf_op jit(solution)/shard_map/ppermute | solution.py:17
  299.9 13.5 %collective-permute-start.3 = (bf16[2,8,128,128]{3,2,1,0:T(8,128)(2,1)S(1)}, bf16[2,8,128,128]{3,2,1,0:T(8,128)(2,1)S(1)}, u32[]{:S(2)}, u32[]{:S(2)}) collective-permute-start(bf16[2,8,128,128]{3,2,1,0:T(8,128)(2,1)S(1)} %slice.14), channel_id=1, source_target_pairs={{0,4},{4,8},{8,12},{12,16},{16,20},{20,24},{24,28},{28,32},{32,36}... | collective-permute-start | bytes 1572872 | tf_op jit(solution)/shard_map/ppermute | solution.py:23
  313.5 2.6 collective-permute-start.4
  314.9 4.4 collective-permute-start.5
  330.4 3.2 copy-start.3
  428.8 6.4 %copy-start.2 = (f32[8,8,8,17,256]{4,2,3,1,0:T(8,128)S(1)}, f32[8,8,8,17,256]{4,2,3,1,0:T(8,128)}, u32[]{:S(2)}) copy-start(f32[8,8,8,17,256]{4,2,3,1,0:T(8,128)} %get-tuple-element.8) | copy-start | bytes 26738692
  441.0 74.1 %copy-start.4 = (f32[256]{0:T(256)S(1)}, f32[256]{0:T(256)}, u32[]{:S(2)}) copy-start(f32[256]{0:T(256)} %param.7) | copy-start | bytes 3076
  441.0 74.1 %copy-start.5 = (f32[256]{0:T(256)S(1)}, f32[256]{0:T(256)}, u32[]{:S(2)}) copy-start(f32[256]{0:T(256)} %param.6) | copy-start | bytes 3076
  594.6 2.5 copy-start.1
where the time goes:
time: 598 us; the launch traced here: 597 us
  waiting for transfers between devices  282 us (47%)
  blocking collectives  197 us (33%)
  local copies, waits for them, and re-layouts  51 us (9%)
  other arithmetic  32.4 us (5%)
  matrix products  19 us (3%)
  starting transfers between devices  15.6 us (3%)
    ppermute x3, waiting for transfers between devices, from_partner(): return lax.ppermute(block, axis, route)  270 us
    psum x1, blocking collectives, per_device(): group_total = lax.psum(local_sums, ('tm', 'rows'))  75.9 us
    psum x1, blocking collectives, per_device(): lax.psum(jnp.sum(centered * centered, axis=(0, 1, 2, 4)), ('tm', 'rows'))  62.4 us
    all_to_all x1, blocking collectives, per_device(): lax.all_to_all(arranged, 'tm', split_axis=1, concat_axis=2, tiled=True)  58.5 us
    conv_general_dilated x6, local copies, waits for them, and re-layouts, per_device(): lax.conv_general_dilated(padded[None], conv_weight, (1, 1, 1), 'VALID', d...  31.9 us
    conv_general_dilated x1, matrix products, per_device(): lax.conv_general_dilated(padded[None], conv_weight, (1, 1, 1), 'VALID', d...  19 us
    reshape x2, local copies, waits for them, and re-layouts, per_device(): arranged.reshape(out_height // 2, out_width // 2, out_frames, 4 * out_cha...  14.1 us
    select_n x2, other arithmetic, per_device(): jnp.where(is_upper, (partner - current) * inv_root, (current + partner) *...  12.8 us
  transfers between devices with their start and end apart: 6, of which 5 were waited for; matrix products, arithmetic and copies ran while one was open for 0% of the time, Pallas kernels for 0%

commit v1 on v0

--- a/solution.py
+++ b/solution.py
@@ -41,6 +41,12 @@
 
 
 def per_device(video, conv_weight, norm_gain, norm_bias):
+
+    def post_the_axis_part(on_dim, along_dim, inputs):
+        w_next = jnp.split(inputs, lax.axis_size("tm"), axis=on_dim)
+        left_arr = lax.all_to_all(jnp.stack(w_next), "tm", 0, 0)
+        return jnp.concatenate(left_arr, axis=along_dim)
+
     frames, height, width, channels = video.shape
     tm_count = lax.axis_size("tm")
     current = video.astype(jnp.float32)
@@ -92,7 +98,7 @@
         out_frames, out_height // 2, 2, out_width // 2, 2, out_channels
     ).transpose(1, 3, 0, 2, 4, 5)
     arranged = arranged.reshape(out_height // 2, out_width // 2, out_frames, 4 * out_channels)
-    return lax.all_to_all(arranged, "tm", split_axis=1, concat_axis=2, tiled=True)
+    return post_the_axis_part(1, 2, arranged)
 
 
 def solution(mesh):

time: 598 us -> 627 us (1.048)
  local copies, waits for them, and re-layouts: 51 us -> 81.2 us
    unnamed x12 -> x43, local copies, waits for them, and re-layouts: 0.03 us -> 28.5 us
    transpose x0 -> x1, local copies, waits for them, and re-layouts: none -> 7.07 us  [per_device(): arranged = activated.reshape(out_frames, out_height // 2, 2, out_width //...]
    reshape x2 -> x1, local copies, waits for them, and re-layouts: 14.1 us -> 7.71 us  [per_device(): arranged.reshape(out_height // 2, out_width // 2, out_frames, 4 * out_cha...]
where the time goes in v1:
time: 627 us; the launch traced here: 625 us
  waiting for transfers between devices  282 us (45%)
  blocking collectives  197 us (31%)
  local copies, waits for them, and re-layouts  81.2 us (13%)
  other arithmetic  30.5 us (5%)
  matrix products  19 us (3%)
  starting transfers between devices  15.6 us (2%)
    ppermute x3, waiting for transfers between devices, from_partner(): return lax.ppermute(block, axis, route)  270 us
    psum x1, blocking collectives, per_device(): group_total = lax.psum(local_sums, ('tm', 'rows'))  75.9 us
    psum x1, blocking collectives, per_device(): lax.psum(jnp.sum(centered * centered, axis=(0, 1, 2, 4)), ('tm', 'rows'))  62.4 us
    all_to_all x1, blocking collectives, post_the_axis_part(): left_arr = lax.all_to_all(jnp.stack(w_next), 'tm', 0, 0)  58.5 us
    conv_general_dilated x6, local copies, waits for them, and re-layouts, per_device(): lax.conv_general_dilated(padded[None], conv_weight, (1, 1, 1), 'VALID', d...  31.9 us
    unnamed x43, local copies, waits for them, and re-layouts  28.5 us
    conv_general_dilated x1, matrix products, per_device(): lax.conv_general_dilated(padded[None], conv_weight, (1, 1, 1), 'VALID', d...  19 us
    select_n x2, other arithmetic, per_device(): jnp.where(is_upper, (partner - current) * inv_root, (current + partner) *...  12.8 us
  transfers between devices with their start and end apart: 6, of which 5 were waited for; matrix products, arithmetic and copies ran while one was open for 0% of the time, Pallas kernels for 0%

profile of v1, /device:TPU:0, one launch (start us, length us, event | category | flops | bytes accessed | tf_op | source)
XLA Modules:
  0.0 625.4 jit_solution(4948978755118399809)
XLA Ops:
  0.0 4.3 convert_element_type.12
  4.3 3.3 collective-permute-start
  7.5 90.9 %collective-permute-done = f32[8,8,128,128]{3,2,1,0:T(8,128)} collective-permute-done((f32[8,8,128,128]{3,2,1,0:T(8,128)}, f32[8,8,128,128]{3,2,1,0:T(8,128)}, u32[]{:S(2)}, u32[]{:S(2)}) %collective-permute-start) | collective-permute-done | bytes 4194336 | tf_op jit(solution)/shard_map/ppermute | solution.py:17
  98.4 5.9 multiply_select_fusion.1
  104.3 1.5 collective-permute-start.1
  105.9 90.2 %collective-permute-done.1 = f32[8,8,128,128]{3,2,1,0:T(8,128)} collective-permute-done((f32[8,8,128,128]{3,2,1,0:T(8,128)}, f32[8,8,128,128]{3,2,1,0:T(8,128)}, u32[]{:S(2)}, u32[]{:S(2)}) %collective-permute-start.1) | collective-permute-done | bytes 4194336 | tf_op jit(solution)/shard_map/ppermute | solution.py:17
  196.1 6.9 %multiply_select_fusion = f32[8,8,128,128]{3,2,1,0:T(8,128)} fusion(f32[8,8,128,128]{3,2,1,0:T(8,128)} %multiply_select_fusion.1, f32[8,8,128,128]{3,2,1,0:T(8,128)} %collective-permute-done.1, pred[]{:T(512)S(6)} %eq.10), kind=kLoop, calls=%fused_computation.11 | loop fusion | flops 5242880 | bytes 12582913 | tf_op jit(solution)/shard_map/jit(_where)/select_n | solution.py:57
  203.0 3.0 collective-permute-start.2
  206.1 89.3 %collective-permute-done.2 = f32[8,8,128,128]{3,2,1,0:T(8,128)} collective-permute-done((f32[8,8,128,128]{3,2,1,0:T(8,128)}, f32[8,8,128,128]{3,2,1,0:T(8,128)}, u32[]{:S(2)}, u32[]{:S(2)}) %collective-permute-start.2) | collective-permute-done | bytes 4194336 | tf_op jit(solution)/shard_map/ppermute | solution.py:17
  295.4 4.5 select_convert_fusion
  299.9 5.1 collective-permute-start.3
  305.1 8.4 %collective-permute-done.3 = bf16[2,8,128,128]{3,2,1,0:T(8,128)(2,1)S(1)} collective-permute-done((bf16[2,8,128,128]{3,2,1,0:T(8,128)(2,1)S(1)}, bf16[2,8,128,128]{3,2,1,0:T(8,128)(2,1)S(1)}, u32[]{:S(2)}, u32[]{:S(2)}) %collective-permute-start.3) | collective-permute-done | bytes 524320 | tf_op jit(solution)/shard_map/ppermute | solution.py:23
  313.5 1.3 collective-permute-start.4
  314.9 1.3 collective-permute-start.5
  316.2 3.1 collective-permute-done.5
  319.3 2.1 fusion.10
  321.4 2.0 pad.5
  323.4 6.9 %reshape.27 = bf16[10,10,1,8,17,128]{5,4,3,1,0,2:T(8,128)(2,1)} reshape(bf16[10,10,1,136,128]{4,3,1,0,2:T(8,128)(2,1)} %pad.5) | data formatting | bytes 6963200 | tf_op jit(solution)/shard_map/conv_general_dilated | solution.py:66
  330.4 3.0 copy.77
  333.5 19.0 %select_reduce_fusion.1 = (f32[256]{0:T(256)S(1)}, f32[8,8,8,17,256]{4,2,3,1,0:T(8,128)}) fusion(pred[8,17]{0,1:T(8,128)(4,1)S(1)} %copy-done.3, bf16[3,3,3,128,256]{4,3,2,1,0:T(8,128)(2,1)S(1)} %copy-done, bf16[10,10,1,7,2,128]{5,3,4,1,0,2:T(8,128)(2,1)S(1)} %slice.15, bf16[10,10,1,8,17,128]{5,3,4,1,0,2:T(8,128)(2,1)S(1)} %copy.77), kind=kOutput, calls=%fused_computation.3 | convolution fusion | flops 15419842560 | bytes 14523528 | tf_op jit(solution)/shard_map/conv_general_dilated | solution.py:66
  352.8 75.9 %psum.14 = f32[32]{0:T(128)S(1)} all-reduce(f32[32]{0:T(128)S(1)} %reduce_sum.25), channel_id=1, replica_groups=mesh['tm'=32,'rows'=4] {'tm','rows'}, use_global_device_ids=true, to_apply=%region_2.3 | all-reduce | flops 32 | bytes 256 | tf_op jit(solution)/shard_map/psum | solution.py:88
  428.9 6.3 %copy.78 = f32[8,8,8,17,256]{4,1,3,2,0:T(8,128)S(1)} copy(f32[8,8,8,17,256]{4,2,3,1,0:T(8,128)} %get-tuple-element.8) | data formatting | bytes 17825792 | tf_op jit(solution)/shard_map/conv_general_dilated | solution.py:66
  435.2 1.5 select_reduce_fusion
  436.8 4.1 slice.16
  441.0 11.5 %copy.79 = f32[8,8,1,128,256]{4,0,3,1,2:T(8,128)} copy(f32[8,8,1,128,256]{4,1,3,0,2:T(8,128)} %slice.16) | data formatting | bytes 16777216 | tf_op jit(solution)/shard_map/conv_general_dilated | solution.py:66
  452.5 62.4 %psum.15 = f32[32]{0:T(128)S(1)} all-reduce(f32[32]{0:T(128)S(1)} %reduce_sum.37), channel_id=1, replica_groups=mesh['tm'=32,'rows'=4] {'tm','rows'}, use_global_device_ids=true, to_apply=%region_5.6 | all-reduce | flops 32 | bytes 256 | tf_op jit(solution)/shard_map/psum | solution.py:91
  515.2 5.0 fusion.2
  520.1 7.1 %copy.80 = bf16[4,64,8,2,2,256]{5,4,3,2,1,0:T(2,128)(2,1)} copy(bf16[4,64,8,2,2,256]{5,2,4,1,3,0:T(8,128)(2,1)S(1)} %fusion.2) | data formatting | bytes 8388608 | tf_op jit(solution)/shard_map/transpose | solution.py:99
  527.2 7.7 %reshape.22 = bf16[4,64,8,1024]{3,2,1,0:T(8,128)(2,1)} reshape(bf16[4,64,8,2,2,256]{5,4,3,2,1,0:T(2,128)(2,1)} %copy.80) | data formatting | bytes 8388608 | tf_op jit(solution)/shard_map/reshape | solution.py:100
  535.8 0.9 fusion.47
  537.7 0.9 fusion.45
  539.5 0.9 fusion.43
  540.4 0.9 fusion.42
  542.3 0.9 fusion.40
  544.1 0.9 fusion.38
  545.1 0.9 fusion.37
  546.0 0.9 fusion.36
  546.9 0.9 fusion.35
  548.7 0.9 fusion.33
  550.6 0.9 fusion.31
  551.5 0.9 fusion.30
  552.4 0.9 fusion.29
  553.4 0.9 fusion.28
  555.2 0.9 fusion.26
  557.0 0.9 fusion.24
  558.0 0.9 fusion.23
  564.4 58.5 %all_to_all.5 = bf16[32,4,2,8,1024]{4,3,2,1,0:T(8,128)(2,1)S(1)} all-to-all(bf16[32,4,2,8,1024]{4,3,2,1,0:T(8,128)(2,1)S(1)} %fusion.17), channel_id=1, replica_groups=mesh['tm'=32,'rows'=4] {'tm'}, dimensions={0} | all-to-all | bytes 8388608 | tf_op jit(solution)/shard_map/all_to_all | solution.py:47
  622.9 2.5 copy_bitcast_fusion
  (41 shorter events, 14.8 us)
Async XLA Ops:
  0.0 333.5 %copy-start = (bf16[3,3,3,128,256]{4,3,2,1,0:T(8,128)(2,1)S(1)}, bf16[3,3,3,128,256]{4,3,2,1,0:T(8,128)(2,1)}, u32[]{:S(2)}) copy-start(bf16[3,3,3,128,256]{4,3,2,1,0:T(8,128)(2,1)} %param.5) | copy-start | bytes 5308420
  4.3 94.2 %collective-permute-start = (f32[8,8,128,128]{3,2,1,0:T(8,128)}, f32[8,8,128,128]{3,2,1,0:T(8,128)}, u32[]{:S(2)}, u32[]{:S(2)}) collective-permute-start(f32[8,8,128,128]{3,2,1,0:T(8,128)} %convert_element_type.12), channel_id=1, source_target_pairs={{0,4},{4,0},{8,12},{12,8},{16,20},{20,16},{24,28},{28,24},{32,36},... | collective-permute-start | bytes 12582920 | tf_op jit(solution)/shard_map/ppermute | solution.py:17
  104.3 91.8 %collective-permute-start.1 = (f32[8,8,128,128]{3,2,1,0:T(8,128)}, f32[8,8,128,128]{3,2,1,0:T(8,128)}, u32[]{:S(2)}, u32[]{:S(2)}) collective-permute-start(f32[8,8,128,128]{3,2,1,0:T(8,128)} %multiply_select_fusion.1), channel_id=1, source_target_pairs={{0,8},{8,0},{4,12},{12,4},{16,24},{24,16},{20,28},{28,20},{32,40},... | collective-permute-start | bytes 12582920 | tf_op jit(solution)/shard_map/ppermute | solution.py:17
  203.0 92.4 %collective-permute-start.2 = (f32[8,8,128,128]{3,2,1,0:T(8,128)}, f32[8,8,128,128]{3,2,1,0:T(8,128)}, u32[]{:S(2)}, u32[]{:S(2)}) collective-permute-start(f32[8,8,128,128]{3,2,1,0:T(8,128)} %multiply_select_fusion), channel_id=1, source_target_pairs={{0,16},{16,0},{4,20},{20,4},{8,24},{24,8},{12,28},{28,12},{32,48},... | collective-permute-start | bytes 12582920 | tf_op jit(solution)/shard_map/ppermute | solution.py:17
  299.9 13.5 %collective-permute-start.3 = (bf16[2,8,128,128]{3,2,1,0:T(8,128)(2,1)S(1)}, bf16[2,8,128,128]{3,2,1,0:T(8,128)(2,1)S(1)}, u32[]{:S(2)}, u32[]{:S(2)}) collective-permute-start(bf16[2,8,128,128]{3,2,1,0:T(8,128)(2,1)S(1)} %slice.14), channel_id=1, source_target_pairs={{0,4},{4,8},{8,12},{12,16},{16,20},{20,24},{24,28},{28,32},{32,36}... | collective-permute-start | bytes 1572872 | tf_op jit(solution)/shard_map/ppermute | solution.py:23
  313.5 2.6 collective-permute-start.4
  314.9 4.4 collective-permute-start.5
  330.4 3.2 copy-start.3
  428.8 6.4 %copy-start.2 = (f32[8,8,8,17,256]{4,2,3,1,0:T(8,128)S(1)}, f32[8,8,8,17,256]{4,2,3,1,0:T(8,128)}, u32[]{:S(2)}) copy-start(f32[8,8,8,17,256]{4,2,3,1,0:T(8,128)} %get-tuple-element.8) | copy-start | bytes 26738692
  441.0 74.1 %copy-start.4 = (f32[256]{0:T(256)S(1)}, f32[256]{0:T(256)}, u32[]{:S(2)}) copy-start(f32[256]{0:T(256)} %param.7) | copy-start | bytes 3076
  441.0 74.1 %copy-start.5 = (f32[256]{0:T(256)S(1)}, f32[256]{0:T(256)}, u32[]{:S(2)}) copy-start(f32[256]{0:T(256)} %param.6) | copy-start | bytes 3076
  564.4 60.9 %copy-start.1 = (bf16[3,3,3,128,256]{4,3,2,1,0:T(8,128)(2,1)S(1)}, bf16[3,3,3,128,256]{4,3,2,1,0:T(8,128)(2,1)}, u32[]{:S(2)}) copy-start(bf16[3,3,3,128,256]{4,3,2,1,0:T(8,128)(2,1)} %param.5) | copy-start | bytes 5308420
